TPU v7x, 32 devices: a whole 2x2x4 slice. The times are simulated.
32 devices in a mesh: gx: 4 (over z), gy: 4 (over y, x), gz: 2 (over core).
Axes of the slice: x: 2, y: 2, z: 4, core: 2. Of those that a mesh axis runs over, the one named last changes fastest.
Arguments:
- populations: float32 [19, 16, 32, 512], P(None, 'gz', 'gx', 'gy'), may hold values from 0.6 to 1.4
- solid_codes: int32 [16, 32, 512], P('gz', 'gx', 'gy'), may hold values from 0 to 8
- plane_offsets: int32 [2, 2], replicated, may hold values from 0 to 31
- plane_fractions: int32 [2, 2], replicated, may hold values from 0 to 63
Outputs:
- populations_next: float32 [19, 16, 32, 512], P(None, 'gz', 'gx', 'gy')
All inputs are finite; a program needn't handle non-finite values.
Results may differ from a plain program's by a relative error of at most 0.0001.
Values sent between devices are 32-bit elements; how exact they have to be, the bound alone decides.
A program may use at most 64 MiB of HBM per device.

v0:
```python
import functools

import jax
import jax.numpy as jnp
from jax import lax
from jax.experimental import pallas as pl
from jax.experimental.pallas import tpu as pltpu
from jax.sharding import PartitionSpec as P

LEVELS = 8
FRAC_DEN = 64
MESH = pl.DeviceIdType.MESH

velocities = (
    (0, 0, 0),
    (1, 0, 0),
    (-1, 0, 0),
    (0, 1, 0),
    (0, -1, 0),
    (0, 0, 1),
    (0, 0, -1),
    (1, 1, 0),
    (-1, -1, 0),
    (1, -1, 0),
    (-1, 1, 0),
    (1, 0, 1),
    (-1, 0, -1),
    (1, 0, -1),
    (-1, 0, 1),
    (0, 1, 1),
    (0, -1, -1),
    (0, 1, -1),
    (0, -1, 1),
)
relax_time = 0.9
rising = (5, 11, 14, 15, 18)
sinking = (6, 12, 13, 16, 17)
x_movers = ((1, 7, 9, 11, 13), (2, 8, 10, 12, 14))
y_movers = ((3, 7, 10, 15, 17), (4, 8, 9, 16, 18))
corners = ((1, 1), (-1, -1), (1, -1), (-1, 1))


def side_of(move):
    return 0 if move > 0 else 1


def collide(pops, codes):
    solid = codes.astype(jnp.float32) * (1.0 / LEVELS)
    sums, diffs = {}, {}
    for i in range(1, 19, 2):
        sums[i] = pops[i] + pops[i + 1]
        diffs[i] = pops[i] - pops[i + 1]
    axis_sum = sums[1] + sums[3] + sums[5]
    diag_sum = (sums[7] + sums[9]) + (sums[11] + sums[13]) + (sums[15] + sums[17])
    density = pops[0] * (1.0 / 3.0) + axis_sum * (1.0 / 18.0) + diag_sum * (1.0 / 36.0)
    flow_x = diffs[1] * 2.0 + ((diffs[7] + diffs[9]) + (diffs[11] + diffs[13]))
    flow_y = diffs[3] * 2.0 + ((diffs[7] - diffs[9]) + (diffs[15] + diffs[17]))
    flow_z = diffs[5] * 2.0 + ((diffs[11] - diffs[13]) + (diffs[15] - diffs[17]))
    inverse = (1.0 / 36.0) / density
    ux, uy, uz = flow_x * inverse, flow_y * inverse, flow_z * inverse
    fluid = 1.0 - solid
    gain = density * fluid * (1.0 / relax_time)
    keep = fluid * (1.0 - 1.0 / relax_time)
    even = 0.5 * (keep + solid)
    odd = 0.5 * (keep - solid)
    rest = gain * (1.0 - 1.5 * (ux * ux + uy * uy + uz * uz))
    gain3, gain45 = gain * 3.0, gain * 4.5
    out = [None] * 19
    out[0] = (keep + solid) * pops[0] + rest
    along = {
        1: ux, 3: uy, 5: uz, 7: ux + uy, 9: ux - uy, 11: ux + uz, 13: ux - uz, 15: uy + uz, 17: uy - uz,
    }
    for i, a in along.items():
        part_even = even * sums[i] + (rest + gain45 * (a * a))
        part_odd = odd * diffs[i] + gain3 * a
        out[i] = part_even + part_odd
        out[i + 1] = part_even - part_odd
    return out


def kernel(
    sizes, off_in, frac_in, pops_in, codes_in, out_to,
    off, frac, pops, codes, out, load_sem, save_sem,
    post, s_strip, s_row, s_col, s_corner, s_edge, r_row, r_col, r_corner, r_edge, send_sem, recv_sem, *r_strip
):
    n_gx, n_gy, n_gz, steps = sizes
    layers, rows, cols = codes.shape
    length = n_gx * rows
    top = layers - 1
    gx, gy, gz = lax.axis_index("gx"), lax.axis_index("gy"), lax.axis_index("gz")
    merged = n_gz == 2
    z_moves = (1,) if merged else (1, -1)

    def peer(move):
        dx, dy, dz = move
        return (
            lax.rem(gx + (dx + n_gx), n_gx),
            lax.rem(gy + (dy + n_gy), n_gy),
            lax.rem(gz + (dz + n_gz), n_gz),
        )

    def messages(step):
        found = []
        for dz in z_moves:
            for k in range(n_gx):
                if merged:
                    src = s_strip.at[step]
                    dst = lambda at: r_strip[step].at[:, :, pl.ds(pl.multiple_of(at * rows, rows), rows), :]
                else:
                    src = s_strip.at[step, side_of(dz)]
                    dst = lambda at, d=side_of(dz): r_strip[step].at[
                        d, :, pl.ds(pl.multiple_of(at * rows, rows), rows), :
                    ]
                found.append(("strip", (k, 0, dz), src, dst))
        for dx in (1, -1):
            d = side_of(dx)
            found.append(("near", (dx, 0, 0), s_row.at[step, d], lambda at, d=d: r_row.at[step, d]))
        for dy in (1, -1):
            d = side_of(dy)
            found.append(("near", (0, dy, 0), s_col.at[step, d], lambda at, d=d: r_col.at[step, d]))
        for c, (dx, dy) in enumerate(corners):
            found.append(
                ("near", (dx, dy, 0), s_corner.at[step, c], lambda at, c=c: r_corner.at[step, c])
            )
        for zi, dz in enumerate(z_moves):
            for dy in (1, -1):
                d = side_of(dy)
                for k in range(n_gx):
                    found.append(
                        (
                            "edge",
                            (k, dy, dz),
                            s_edge.at[step, d],
                            lambda at, zi=zi, d=d: r_edge.at[step, zi, d, at],
                        )
                    )
        return found

    def copy_of(step, number, entry, incoming):
        group, move, src, dst = entry
        at = lax.rem(gx - move[0] + n_gx, n_gx) if incoming else gx
        return pltpu.make_async_remote_copy(
            src_ref=src,
            dst_ref=dst(at),
            send_sem=send_sem.at[step, number],
            recv_sem=recv_sem.at[step, number],
            device_id=peer(move),
            device_id_type=MESH,
        )

    def start(step, group):
        for number, entry in enumerate(messages(step)):
            if entry[0] == group:
                copy_of(step, number, entry, False).start()

    def arrive(step, group):
        for number, entry in enumerate(messages(step)):
            if entry[0] == group:
                copy_of(step, number, entry, True).wait_recv()

    def finish(step):
        for number, entry in enumerate(messages(step)):
            copy_of(step, number, entry, False).wait_send()

    inside = pl.ds(1, layers - 2)
    loads = [
        pltpu.make_async_copy(src, dst, load_sem.at[number])
        for number, (src, dst) in enumerate(
            (
                (codes_in, codes),
                (pops_in.at[:, 0], pops.at[:, 0]),
                (pops_in.at[:, top], pops.at[:, top]),
                (pops_in.at[:, inside], pops.at[:, inside]),
                (off_in, off),
                (frac_in, frac),
            )
        )
    ]
    for load in loads:
        load.start()

    moves = sorted({tuple(m % n for m, n in zip(entry[1], (n_gx, n_gy, n_gz))) for entry in messages(0)})
    barrier = pltpu.get_barrier_semaphore()
    for move in moves:
        pl.semaphore_signal(barrier, inc=1, device_id=peer(move), device_id_type=MESH)

    lane = lax.broadcasted_iota(jnp.int32, (rows, cols), 1)
    sub = lax.broadcasted_iota(jnp.int32, (rows, cols), 0)

    def to_lane(value, origin, target):
        return pltpu.roll(value, lax.rem(target - origin + 2 * cols, cols), 1)

    def publish(step, z, after, packed):
        for i in range(19):
            post[step, i, z] = after[i]
        for d in (0, 1):
            edge = rows - 1 if d == 0 else 0
            for j, i in enumerate(x_movers[d]):
                s_row[step, d, j, pl.ds(z, 1), :] = after[i][edge : edge + 1, :]
        result = []
        for d in (0, 1):
            value = packed[d]
            edge = cols - 1 if d == 0 else 0
            for j, i in enumerate(y_movers[d]):
                place = j * layers + z
                value = jnp.where(lane == place, to_lane(after[i], edge, place), value)
            result.append(value)
        return tuple(result)

    def publish_strips(step, bottom_after, top_after):
        for j, i in enumerate(rising):
            s_strip[step, 0, j] = top_after[i]
        for j, i in enumerate(sinking):
            s_strip[step, 1, j] = bottom_after[i]
        for d in (0, 1):
            dy = 1 if d == 0 else -1
            edge = cols - 1 if d == 0 else 0
            (up,) = [i for i in rising if velocities[i][1] == dy]
            (down,) = [i for i in sinking if velocities[i][1] == dy]
            place = gx * rows + sub
            spread = jnp.where(lane == place, top_after[up][:, edge : edge + 1], 0.0)
            spread = jnp.where(lane == place + length, bottom_after[down][:, edge : edge + 1], spread)
            s_edge[step, d] = jnp.sum(spread, axis=0, keepdims=True)

    def send(step, packed):
        for d in (0, 1):
            s_col[step, d] = packed[d]
        for c, (dx, dy) in enumerate(corners):
            edge = rows - 1 if dx > 0 else 0
            s_corner[step, c] = packed[side_of(dy)][edge : edge + 1, :]
        start(step, "near")
        start(step, "strip")
        start(step, "edge")

    def crossing(step, side, j, i):
        dx, dy, _ = velocities[i]
        if side == 0:
            plane = gz
            near = gx * rows - dx - off[step, plane]
            far = near - 1
        else:
            plane = lax.rem(gz + 1, n_gz)
            near = gx * rows - dx + off[step, plane]
            far = near + 1
        near = lax.rem(near + 2 * length, length)
        far = lax.rem(far + 2 * length, length)
        weight = frac[step, plane].astype(jnp.float32) * (1.0 / FRAC_DEN)
        value = (1.0 - weight) * r_strip[step][side, j, pl.ds(near, rows), :]
        value = value + weight * r_strip[step][side, j, pl.ds(far, rows), :]
        if dy == 0:
            return value
        d = side_of(dy)
        zi = 0 if merged else side
        gathered = r_edge[step, zi, d, 0]
        for k in range(1, n_gx):
            gathered = gathered + r_edge[step, zi, d, k]
        place_near, place_far = near + sub, far + sub
        place_near = jnp.where(place_near >= length, place_near - length, place_near) + side * length
        place_far = jnp.where(place_far >= length, place_far - length, place_far) + side * length
        picked = jnp.where(lane == place_near, 1.0 - weight, 0.0) + jnp.where(lane == place_far, weight, 0.0)
        halo = jnp.sum(gathered * picked, axis=1, keepdims=True)
        target = 0 if dy > 0 else cols - 1
        return jnp.where(lane == target, halo, pltpu.roll(value, dy % cols, 1))

    def halo_columns(step):
        found = {}
        for dy in (1, -1):
            found[0, dy] = r_col[step, side_of(dy)]
        for c, (dx, dy) in enumerate(corners):
            edge = 0 if dx > 0 else rows - 1
            found[dx, dy] = jnp.where(
                sub == edge, r_corner[step, c], pltpu.roll(found[0, dy], dx % rows, 0)
            )
        return found

    def passed(step, z, halos, edge_layer):
        arrived = []
        for i in range(19):
            dx, dy, dz = velocities[i]
            if edge_layer == 0 and dz == 1:
                arrived.append(crossing(step, 0, rising.index(i), i))
                continue
            if edge_layer == top and dz == -1:
                arrived.append(crossing(step, 1, sinking.index(i), i))
                continue
            origin = z - dz
            value = post[step, i, origin]
            if dx:
                d = side_of(dx)
                edge = 0 if dx > 0 else rows - 1
                row = r_row[step, d, x_movers[d].index(i), pl.ds(origin, 1), :]
                value = jnp.where(sub == edge, row, pltpu.roll(value, dx % rows, 0))
            if dy:
                target = 0 if dy > 0 else cols - 1
                place = y_movers[side_of(dy)].index(i) * layers + origin
                value = jnp.where(
                    lane == target, to_lane(halos[dx, dy], place, target), pltpu.roll(value, dy % cols, 1)
                )
            arrived.append(value)
        return arrived

    def wrap_rows(step):
        for side in (0, 1):
            for j in range(5):
                r_strip[step][side, j, pl.ds(length, 2 * rows), :] = r_strip[step][side, j, pl.ds(0, 2 * rows), :]

    def inner(body, carry):
        for z in range(1, top):
            carry = body(z, carry)
        return carry

    nothing = (jnp.zeros((rows, cols), jnp.float32),) * 2

    packed = nothing
    ends = {}
    loads[0].wait()
    for number, z in ((1, 0), (2, top)):
        loads[number].wait()
        ends[z] = collide([pops[i, z] for i in range(19)], codes[z])
        packed = publish(0, z, ends[z], packed)
    publish_strips(0, ends[0], ends[top])
    loads[3].wait()

    def first(z, packed):
        return publish(0, z, collide([pops[i, z] for i in range(19)], codes[z]), packed)

    packed = inner(first, packed)
    pl.semaphore_wait(barrier, len(moves))
    send(0, packed)
    loads[4].wait()
    loads[5].wait()

    for step in range(1, steps):
        arrive(step - 1, "near")
        halos = halo_columns(step - 1)

        def middle(z, packed, step=step, halos=halos):
            return publish(step, z, collide(passed(step - 1, z, halos, None), codes[z]), packed)

        packed = inner(middle, nothing)
        arrive(step - 1, "strip")
        arrive(step - 1, "edge")
        wrap_rows(step - 1)
        for z in (0, top):
            ends[z] = collide(passed(step - 1, z, halos, z), codes[z])
            packed = publish(step, z, ends[z], packed)
        publish_strips(step, ends[0], ends[top])
        send(step, packed)

    arrive(steps - 1, "near")
    halos = halo_columns(steps - 1)

    def last(z, carry):
        for i, value in enumerate(passed(steps - 1, z, halos, None)):
            out[i, z] = value
        return carry

    inner(last, 0)
    saves = [pltpu.make_async_copy(out.at[:, inside], out_to.at[:, inside], save_sem.at[0])]
    saves[0].start()
    arrive(steps - 1, "strip")
    arrive(steps - 1, "edge")
    wrap_rows(steps - 1)
    for z in (0, top):
        for i, value in enumerate(passed(steps - 1, z, halos, z)):
            out[i, z] = value
        saves.append(pltpu.make_async_copy(out.at[:, z], out_to.at[:, z], save_sem.at[len(saves)]))
        saves[-1].start()
    for step in range(steps):
        finish(step)
    for save in saves:
        save.wait()


def body(sizes, populations, solid_codes, plane_offsets, plane_fractions):
    n_gx, n_gy, n_gz = sizes
    _, layers, rows, cols = populations.shape
    steps = plane_offsets.shape[0]
    n_z = 1 if n_gz == 2 else 2
    gathered = n_gx * rows + 2 * rows
    n_messages = n_z * n_gx + 2 + 2 + 4 + n_z * 2 * n_gx
    f32 = jnp.float32
    return pl.pallas_call(
        functools.partial(kernel, (n_gx, n_gy, n_gz, steps)),
        out_shape=jax.ShapeDtypeStruct(populations.shape, f32),
        in_specs=[
            pl.BlockSpec(memory_space=pltpu.HBM),
            pl.BlockSpec(memory_space=pltpu.HBM),
            pl.BlockSpec(memory_space=pltpu.HBM),
            pl.BlockSpec(memory_space=pltpu.HBM),
        ],
        out_specs=pl.BlockSpec(memory_space=pltpu.HBM),
        scratch_shapes=[
            pltpu.SMEM(plane_offsets.shape, jnp.int32),
            pltpu.SMEM(plane_fractions.shape, jnp.int32),
            pltpu.VMEM(populations.shape, f32),
            pltpu.VMEM(solid_codes.shape, jnp.int32),
            pltpu.VMEM(populations.shape, f32),
            pltpu.SemaphoreType.DMA((6,)),
            pltpu.SemaphoreType.DMA((3,)),
            pltpu.VMEM((steps, 19, layers, rows, cols), f32),
            pltpu.VMEM((steps, 2, 5, rows, cols), f32),
            pltpu.VMEM((steps, 2, 5, layers, cols), f32),
            pltpu.VMEM((steps, 2, rows, cols), f32),
            pltpu.VMEM((steps, 4, 1, cols), f32),
            pltpu.VMEM((steps, 2, 1, cols), f32),
            pltpu.VMEM((steps, 2, 5, layers, cols), f32),
            pltpu.VMEM((steps, 2, rows, cols), f32),
            pltpu.VMEM((steps, 4, 1, cols), f32),
            pltpu.VMEM((steps, n_z, 2, n_gx, 1, cols), f32),
            pltpu.SemaphoreType.DMA((steps, n_messages)),
            pltpu.SemaphoreType.DMA((steps, n_messages)),
        ]
        + [pltpu.VMEM((2, 5, gathered, cols), f32)] * steps,
        compiler_params=pltpu.CompilerParams(
            collective_id=0, has_side_effects=True, vmem_limit_bytes=60 * 1024 * 1024
        ),
    )(plane_offsets, plane_fractions, populations, solid_codes)


def solution(mesh):
    sizes = tuple(mesh.shape[name] for name in ("gx", "gy", "gz"))
    in_specs = (P(None, "gz", "gx", "gy"), P("gz", "gx", "gy"), P(), P())
    out_specs = P(None, "gz", "gx", "gy")
    return jax.shard_map(
        functools.partial(body, sizes), mesh=mesh, in_specs=in_specs, out_specs=out_specs, check_vma=False
    )
```

profile of v0, /device:TPU:0, one launch (start us, length us, event | category | flops | bytes accessed | tf_op | source)
XLA Modules:
  0.0 24.9 jit_solution(18145892298642809740)
XLA Ops:
  0.0 22.9 %shard_map.46 = f32[19,8,8,128]{3,2,1,0:T(8,128)} custom-call(s32[2,2]{1,0:T(2,128)} %off_in.1, s32[2,2]{1,0:T(2,128)} %frac_in.1, f32[19,8,8,128]{3,2,1,0:T(8,128)} %pops_in.1, s32[8,8,128]{2,1,0:T(8,128)} %codes_in.1), custom_call_target="tpu_custom_call" | custom-call | tf_op jit(solution)/shard_map/pallas_call | solution.py:383
  22.9 2.0 %copy.6 = f32[19,8,8,128]{3,2,1,0:T(8,128)} copy(f32[19,8,8,128]{3,2,1,0:T(8,128)} %shard_map.46) | data formatting | bytes 1245184
where the time goes:
time: 25.1 us; the launch traced here: 24.9 us
  Pallas kernels  22.9 us (91%)
  local copies, waits for them, and re-layouts  1.96 us (8%)
    pallas_call x1, Pallas kernels, body(): pl.pallas_call(functools.partial(kernel, (n_gx, n_gy, n_gz, steps)), out_...  22.9 us
    unnamed x1, local copies, waits for them, and re-layouts  1.96 us

commit v1 on v0

--- a/solution.py
+++ b/solution.py
@@ -81,9 +81,11 @@
 def kernel(
     sizes, off_in, frac_in, pops_in, codes_in, out_to,
     off, frac, pops, codes, out, load_sem, save_sem,
-    post, s_strip, s_row, s_col, s_corner, s_edge, r_row, r_col, r_corner, r_edge, send_sem, recv_sem, *r_strip
+    post, s_strip, s_inner, s_end, s_col, s_corner, s_edge,
+    r_inner, r_end, r_col, r_corner, r_edge, send_sem, recv_sem, *gathers
 ):
     n_gx, n_gy, n_gz, steps = sizes
+    r_strip = [gathers[2 * step : 2 * step + 2] for step in range(steps)]
     layers, rows, cols = codes.shape
     length = n_gx * rows
     top = layers - 1
@@ -101,20 +103,22 @@
 
     def messages(step):
         found = []
-        for dz in z_moves:
+        for side, dz in ((0, 1), (1, -1)):
             for k in range(n_gx):
-                if merged:
-                    src = s_strip.at[step]
-                    dst = lambda at: r_strip[step].at[:, :, pl.ds(pl.multiple_of(at * rows, rows), rows), :]
-                else:
-                    src = s_strip.at[step, side_of(dz)]
-                    dst = lambda at, d=side_of(dz): r_strip[step].at[
-                        d, :, pl.ds(pl.multiple_of(at * rows, rows), rows), :
-                    ]
-                found.append(("strip", (k, 0, dz), src, dst))
+                found.append(
+                    (
+                        ("rise", "sink")[side],
+                        (k, 0, dz),
+                        s_strip.at[step, side],
+                        lambda at, side=side: r_strip[step][side].at[
+                            :, pl.ds(pl.multiple_of(at * rows, rows), rows), :
+                        ],
+                    )
+                )
         for dx in (1, -1):
             d = side_of(dx)
-            found.append(("near", (dx, 0, 0), s_row.at[step, d], lambda at, d=d: r_row.at[step, d]))
+            found.append(("inner", (dx, 0, 0), s_inner.at[step, d], lambda at, d=d: r_inner.at[step, d]))
+            found.append(("near", (dx, 0, 0), s_end.at[step, d], lambda at, d=d: r_end.at[step, d]))
         for dy in (1, -1):
             d = side_of(dy)
             found.append(("near", (0, dy, 0), s_col.at[step, d], lambda at, d=d: r_col.at[step, d]))
@@ -196,7 +200,13 @@
         for d in (0, 1):
             edge = rows - 1 if d == 0 else 0
             for j, i in enumerate(x_movers[d]):
-                s_row[step, d, j, pl.ds(z, 1), :] = after[i][edge : edge + 1, :]
+                row = after[i][edge : edge + 1, :]
+                if 0 < z < top:
+                    place = (z - 1) * 5 + j
+                    s_inner[step, d, place : place + 1, :] = row
+                else:
+                    place = j if z == 0 else 8 + j
+                    s_end[step, d, place : place + 1, :] = row
         result = []
         for d in (0, 1):
             value = packed[d]
@@ -207,11 +217,11 @@
             result.append(value)
         return tuple(result)
 
-    def publish_strips(step, bottom_after, top_after):
-        for j, i in enumerate(rising):
-            s_strip[step, 0, j] = top_after[i]
-        for j, i in enumerate(sinking):
-            s_strip[step, 1, j] = bottom_after[i]
+    def publish_strip(step, side, after):
+        for j, i in enumerate((rising, sinking)[side]):
+            s_strip[step, side, j] = after[i]
+
+    def publish_edges(step, bottom_after, top_after):
         for d in (0, 1):
             dy = 1 if d == 0 else -1
             edge = cols - 1 if d == 0 else 0
@@ -222,15 +232,12 @@
             spread = jnp.where(lane == place + length, bottom_after[down][:, edge : edge + 1], spread)
             s_edge[step, d] = jnp.sum(spread, axis=0, keepdims=True)
 
-    def send(step, packed):
+    def publish_columns(step, packed):
         for d in (0, 1):
             s_col[step, d] = packed[d]
         for c, (dx, dy) in enumerate(corners):
             edge = rows - 1 if dx > 0 else 0
             s_corner[step, c] = packed[side_of(dy)][edge : edge + 1, :]
-        start(step, "near")
-        start(step, "strip")
-        start(step, "edge")
 
     def crossing(step, side, j, i):
         dx, dy, _ = velocities[i]
@@ -245,8 +252,8 @@
         near = lax.rem(near + 2 * length, length)
         far = lax.rem(far + 2 * length, length)
         weight = frac[step, plane].astype(jnp.float32) * (1.0 / FRAC_DEN)
-        value = (1.0 - weight) * r_strip[step][side, j, pl.ds(near, rows), :]
-        value = value + weight * r_strip[step][side, j, pl.ds(far, rows), :]
+        value = (1.0 - weight) * r_strip[step][side][j, pl.ds(near, rows), :]
+        value = value + weight * r_strip[step][side][j, pl.ds(far, rows), :]
         if dy == 0:
             return value
         d = side_of(dy)
@@ -288,7 +295,11 @@
             if dx:
                 d = side_of(dx)
                 edge = 0 if dx > 0 else rows - 1
-                row = r_row[step, d, x_movers[d].index(i), pl.ds(origin, 1), :]
+                j = x_movers[d].index(i)
+                if 0 < origin < top:
+                    row = r_inner[step, d, pl.ds((origin - 1) * 5 + j, 1), :]
+                else:
+                    row = r_end[step, d, pl.ds(j if origin == 0 else 8 + j, 1), :]
                 value = jnp.where(sub == edge, row, pltpu.roll(value, dx % rows, 0))
             if dy:
                 target = 0 if dy > 0 else cols - 1
@@ -299,10 +310,9 @@
             arrived.append(value)
         return arrived
 
-    def wrap_rows(step):
-        for side in (0, 1):
-            for j in range(5):
-                r_strip[step][side, j, pl.ds(length, 2 * rows), :] = r_strip[step][side, j, pl.ds(0, 2 * rows), :]
+    def wrap_rows(step, side):
+        for j in range(5):
+            r_strip[step][side][j, pl.ds(length, 2 * rows), :] = r_strip[step][side][j, pl.ds(0, 2 * rows), :]
 
     def inner(body, carry):
         for z in range(1, top):
@@ -318,19 +328,26 @@
         loads[number].wait()
         ends[z] = collide([pops[i, z] for i in range(19)], codes[z])
         packed = publish(0, z, ends[z], packed)
-    publish_strips(0, ends[0], ends[top])
+    publish_strip(0, 0, ends[top])
+    publish_strip(0, 1, ends[0])
+    publish_edges(0, ends[0], ends[top])
+    pl.semaphore_wait(barrier, len(moves))
+    start(0, "edge")
+    start(0, "rise")
     loads[3].wait()
 
     def first(z, packed):
         return publish(0, z, collide([pops[i, z] for i in range(19)], codes[z]), packed)
 
-    packed = inner(first, packed)
-    pl.semaphore_wait(barrier, len(moves))
-    send(0, packed)
+    publish_columns(0, inner(first, packed))
+    start(0, "inner")
+    start(0, "near")
+    start(0, "sink")
     loads[4].wait()
     loads[5].wait()
 
     for step in range(1, steps):
+        arrive(step - 1, "inner")
         arrive(step - 1, "near")
         halos = halo_columns(step - 1)
 
@@ -338,31 +355,42 @@
             return publish(step, z, collide(passed(step - 1, z, halos, None), codes[z]), packed)
 
         packed = inner(middle, nothing)
-        arrive(step - 1, "strip")
+        start(step, "inner")
         arrive(step - 1, "edge")
-        wrap_rows(step - 1)
-        for z in (0, top):
-            ends[z] = collide(passed(step - 1, z, halos, z), codes[z])
-            packed = publish(step, z, ends[z], packed)
-        publish_strips(step, ends[0], ends[top])
-        send(step, packed)
-
-    arrive(steps - 1, "near")
-    halos = halo_columns(steps - 1)
+        arrive(step - 1, "rise")
+        wrap_rows(step - 1, 0)
+        ends[0] = collide(passed(step - 1, 0, halos, 0), codes[0])
+        publish_strip(step, 1, ends[0])
+        start(step, "sink")
+        packed = publish(step, 0, ends[0], packed)
+        arrive(step - 1, "sink")
+        wrap_rows(step - 1, 1)
+        ends[top] = collide(passed(step - 1, top, halos, top), codes[top])
+        publish_strip(step, 0, ends[top])
+        publish_edges(step, ends[0], ends[top])
+        start(step, "edge")
+        start(step, "rise")
+        publish_columns(step, publish(step, top, ends[top], packed))
+        start(step, "near")
+
+    step = steps - 1
+    arrive(step, "inner")
+    arrive(step, "near")
+    halos = halo_columns(step)
 
     def last(z, carry):
-        for i, value in enumerate(passed(steps - 1, z, halos, None)):
+        for i, value in enumerate(passed(step, z, halos, None)):
             out[i, z] = value
         return carry
 
     inner(last, 0)
     saves = [pltpu.make_async_copy(out.at[:, inside], out_to.at[:, inside], save_sem.at[0])]
     saves[0].start()
-    arrive(steps - 1, "strip")
-    arrive(steps - 1, "edge")
-    wrap_rows(steps - 1)
-    for z in (0, top):
-        for i, value in enumerate(passed(steps - 1, z, halos, z)):
+    arrive(step, "edge")
+    for side, z in ((1, top), (0, 0)):
+        arrive(step, ("rise", "sink")[side])
+        wrap_rows(step, side)
+        for i, value in enumerate(passed(step, z, halos, z)):
             out[i, z] = value
         saves.append(pltpu.make_async_copy(out.at[:, z], out_to.at[:, z], save_sem.at[len(saves)]))
         saves[-1].start()
@@ -372,15 +400,29 @@
         save.wait()
 
 
+def hand_over(chunks, source, target, sem):
+    count = source.shape[0]
+    cuts = [count * c // chunks for c in range(chunks + 1)]
+    copies = []
+    for c in range(chunks):
+        part = pl.ds(cuts[c], cuts[c + 1] - cuts[c])
+        copies.append(pltpu.make_async_copy(source.at[part], target.at[part], sem.at[c]))
+    for copy in copies:
+        copy.start()
+    for copy in copies:
+        copy.wait()
+
+
 def body(sizes, populations, solid_codes, plane_offsets, plane_fractions):
     n_gx, n_gy, n_gz = sizes
     _, layers, rows, cols = populations.shape
     steps = plane_offsets.shape[0]
     n_z = 1 if n_gz == 2 else 2
     gathered = n_gx * rows + 2 * rows
-    n_messages = n_z * n_gx + 2 + 2 + 4 + n_z * 2 * n_gx
+    n_messages = 2 * n_gx + 2 * 2 + 2 + 4 + n_z * 2 * n_gx
+    inner_rows = -(-5 * (layers - 2) // 8) * 8
     f32 = jnp.float32
-    return pl.pallas_call(
+    moved = pl.pallas_call(
         functools.partial(kernel, (n_gx, n_gy, n_gz, steps)),
         out_shape=jax.ShapeDtypeStruct(populations.shape, f32),
         in_specs=[
@@ -400,22 +442,33 @@
             pltpu.SemaphoreType.DMA((3,)),
             pltpu.VMEM((steps, 19, layers, rows, cols), f32),
             pltpu.VMEM((steps, 2, 5, rows, cols), f32),
-            pltpu.VMEM((steps, 2, 5, layers, cols), f32),
+            pltpu.VMEM((steps, 2, inner_rows, cols), f32),
+            pltpu.VMEM((steps, 2, 16, cols), f32),
             pltpu.VMEM((steps, 2, rows, cols), f32),
             pltpu.VMEM((steps, 4, 1, cols), f32),
             pltpu.VMEM((steps, 2, 1, cols), f32),
-            pltpu.VMEM((steps, 2, 5, layers, cols), f32),
+            pltpu.VMEM((steps, 2, inner_rows, cols), f32),
+            pltpu.VMEM((steps, 2, 16, cols), f32),
             pltpu.VMEM((steps, 2, rows, cols), f32),
             pltpu.VMEM((steps, 4, 1, cols), f32),
             pltpu.VMEM((steps, n_z, 2, n_gx, 1, cols), f32),
             pltpu.SemaphoreType.DMA((steps, n_messages)),
             pltpu.SemaphoreType.DMA((steps, n_messages)),
         ]
-        + [pltpu.VMEM((2, 5, gathered, cols), f32)] * steps,
+        + [pltpu.VMEM((5, gathered, cols), f32)] * (2 * steps),
         compiler_params=pltpu.CompilerParams(
             collective_id=0, has_side_effects=True, vmem_limit_bytes=60 * 1024 * 1024
         ),
     )(plane_offsets, plane_fractions, populations, solid_codes)
+    chunks = 7
+    return pl.pallas_call(
+        functools.partial(hand_over, chunks),
+        out_shape=jax.ShapeDtypeStruct(populations.shape, f32),
+        in_specs=[pl.BlockSpec(memory_space=pltpu.HBM)],
+        out_specs=pl.BlockSpec(memory_space=pltpu.HBM),
+        scratch_shapes=[pltpu.SemaphoreType.DMA((chunks,))],
+        compiler_params=pltpu.CompilerParams(vmem_limit_bytes=60 * 1024 * 1024),
+    )(moved)
 
 
 def solution(mesh):

time: 25.1 us -> 42.5 us (1.69)
  Pallas kernels: 22.9 us -> 42.4 us
  local copies, waits for them, and re-layouts: 1.96 us -> 0 us
    pallas_call x0 -> x1, Pallas kernels: none -> 20 us  [body(): pl.pallas_call(functools.partial(hand_over, chunks), out_shape=jax.ShapeD...]
    unnamed x1 -> x0, local copies, waits for them, and re-layouts: 1.96 us -> none
    pallas_call x1, Pallas kernels: 22.9 us -> 22.4 us  [body(): pl.pallas_call(functools.partial(kernel, (n_gx, n_gy, n_gz, steps)), out_...]
where the time goes in v1:
time: 42.5 us; the launch traced here: 42.4 us
  Pallas kernels  42.4 us (100%)
    pallas_call x1, Pallas kernels, body(): pl.pallas_call(functools.partial(kernel, (n_gx, n_gy, n_gz, steps)), out_...  22.4 us
    pallas_call x1, Pallas kernels, body(): pl.pallas_call(functools.partial(hand_over, chunks), out_shape=jax.ShapeD...  20 us

profile of v1, /device:TPU:0, one launch (start us, length us, event | category | flops | bytes accessed | tf_op | source)
XLA Modules:
  0.0 42.4 jit_solution(14975779699420106569)
XLA Ops:
  0.0 22.4 %shard_map.46.source = f32[19,8,8,128]{3,2,1,0:T(8,128)} custom-call(s32[2,2]{1,0:T(2,128)} %off_in.1, s32[2,2]{1,0:T(2,128)} %frac_in.1, f32[19,8,8,128]{3,2,1,0:T(8,128)} %pops_in.1, s32[8,8,128]{2,1,0:T(8,128)} %codes_in.1), custom_call_target="tpu_custom_call" | custom-call | tf_op jit(solution)/shard_map/pallas_call | solution.py:425
  22.4 20.0 %shard_map.47 = f32[19,8,8,128]{3,2,1,0:T(8,128)} custom-call(f32[19,8,8,128]{3,2,1,0:T(8,128)} %shard_map.46.source), custom_call_target="tpu_custom_call" | custom-call | tf_op jit(solution)/shard_map/pallas_call | solution.py:464

commit v2 on v1

--- a/solution.py
+++ b/solution.py
@@ -37,6 +37,8 @@
 sinking = (6, 12, 13, 16, 17)
 x_movers = ((1, 7, 9, 11, 13), (2, 8, 10, 12, 14))
 y_movers = ((3, 7, 10, 15, 17), (4, 8, 9, 16, 18))
+x_bottom = ((1, 7, 9, 11), (2, 8, 10, 14))
+x_top = ((1, 7, 9, 13), (2, 8, 10, 12))
 corners = ((1, 1), (-1, -1), (1, -1), (-1, 1))
 
 
@@ -162,9 +164,10 @@
             if entry[0] == group:
                 copy_of(step, number, entry, True).wait_recv()
 
-    def finish(step):
+    def finish(step, groups):
         for number, entry in enumerate(messages(step)):
-            copy_of(step, number, entry, False).wait_send()
+            if entry[0] in groups:
+                copy_of(step, number, entry, False).wait_send()
 
     inside = pl.ds(1, layers - 2)
     loads = [
@@ -199,14 +202,15 @@
             post[step, i, z] = after[i]
         for d in (0, 1):
             edge = rows - 1 if d == 0 else 0
-            for j, i in enumerate(x_movers[d]):
-                row = after[i][edge : edge + 1, :]
-                if 0 < z < top:
-                    place = (z - 1) * 5 + j
-                    s_inner[step, d, place : place + 1, :] = row
-                else:
-                    place = j if z == 0 else 8 + j
-                    s_end[step, d, place : place + 1, :] = row
+            if 0 < z < top:
+                target, first_row, movers = s_inner, (z - 1) * 5, x_movers[d]
+            elif z == 0:
+                target, first_row, movers = s_end, 0, x_bottom[d]
+            else:
+                target, first_row, movers = s_end, 4, x_top[d]
+            for j, i in enumerate(movers):
+                place = first_row + j
+                target[step, d, place : place + 1, :] = after[i][edge : edge + 1, :]
         result = []
         for d in (0, 1):
             value = packed[d]
@@ -295,11 +299,12 @@
             if dx:
                 d = side_of(dx)
                 edge = 0 if dx > 0 else rows - 1
-                j = x_movers[d].index(i)
                 if 0 < origin < top:
-                    row = r_inner[step, d, pl.ds((origin - 1) * 5 + j, 1), :]
+                    row = r_inner[step, d, pl.ds((origin - 1) * 5 + x_movers[d].index(i), 1), :]
+                elif origin == 0:
+                    row = r_end[step, d, pl.ds(x_bottom[d].index(i), 1), :]
                 else:
-                    row = r_end[step, d, pl.ds(j if origin == 0 else 8 + j, 1), :]
+                    row = r_end[step, d, pl.ds(4 + x_top[d].index(i), 1), :]
                 value = jnp.where(sub == edge, row, pltpu.roll(value, dx % rows, 0))
             if dy:
                 target = 0 if dy > 0 else cols - 1
@@ -342,6 +347,7 @@
     publish_columns(0, inner(first, packed))
     start(0, "inner")
     start(0, "near")
+    finish(0, ("rise",))
     start(0, "sink")
     loads[4].wait()
     loads[5].wait()
@@ -394,23 +400,28 @@
             out[i, z] = value
         saves.append(pltpu.make_async_copy(out.at[:, z], out_to.at[:, z], save_sem.at[len(saves)]))
         saves[-1].start()
-    for step in range(steps):
-        finish(step)
+    finish(0, ("sink", "inner", "near", "edge"))
+    for step in range(1, steps):
+        finish(step, ("rise", "sink", "inner", "near", "edge"))
     for save in saves:
         save.wait()
 
 
-def hand_over(chunks, source, target, sem):
+def hand_over(chunks, source, target, held, load_sem, save_sem):
     count = source.shape[0]
     cuts = [count * c // chunks for c in range(chunks + 1)]
-    copies = []
+    loads, saves = [], []
     for c in range(chunks):
         part = pl.ds(cuts[c], cuts[c + 1] - cuts[c])
-        copies.append(pltpu.make_async_copy(source.at[part], target.at[part], sem.at[c]))
-    for copy in copies:
-        copy.start()
-    for copy in copies:
-        copy.wait()
+        loads.append(pltpu.make_async_copy(source.at[part], held.at[part], load_sem.at[c]))
+        saves.append(pltpu.make_async_copy(held.at[part], target.at[part], save_sem.at[c]))
+    for load in loads:
+        load.start()
+    for load, save in zip(loads, saves):
+        load.wait()
+        save.start()
+    for save in saves:
+        save.wait()
 
 
 def body(sizes, populations, solid_codes, plane_offsets, plane_fractions):
@@ -443,12 +454,12 @@
             pltpu.VMEM((steps, 19, layers, rows, cols), f32),
             pltpu.VMEM((steps, 2, 5, rows, cols), f32),
             pltpu.VMEM((steps, 2, inner_rows, cols), f32),
-            pltpu.VMEM((steps, 2, 16, cols), f32),
+            pltpu.VMEM((steps, 2, 8, cols), f32),
             pltpu.VMEM((steps, 2, rows, cols), f32),
             pltpu.VMEM((steps, 4, 1, cols), f32),
             pltpu.VMEM((steps, 2, 1, cols), f32),
             pltpu.VMEM((steps, 2, inner_rows, cols), f32),
-            pltpu.VMEM((steps, 2, 16, cols), f32),
+            pltpu.VMEM((steps, 2, 8, cols), f32),
             pltpu.VMEM((steps, 2, rows, cols), f32),
             pltpu.VMEM((steps, 4, 1, cols), f32),
             pltpu.VMEM((steps, n_z, 2, n_gx, 1, cols), f32),
@@ -460,13 +471,17 @@
             collective_id=0, has_side_effects=True, vmem_limit_bytes=60 * 1024 * 1024
         ),
     )(plane_offsets, plane_fractions, populations, solid_codes)
-    chunks = 7
+    chunks = 4
     return pl.pallas_call(
         functools.partial(hand_over, chunks),
         out_shape=jax.ShapeDtypeStruct(populations.shape, f32),
         in_specs=[pl.BlockSpec(memory_space=pltpu.HBM)],
         out_specs=pl.BlockSpec(memory_space=pltpu.HBM),
-        scratch_shapes=[pltpu.SemaphoreType.DMA((chunks,))],
+        scratch_shapes=[
+            pltpu.VMEM(populations.shape, f32),
+            pltpu.SemaphoreType.DMA((chunks,)),
+            pltpu.SemaphoreType.DMA((chunks,)),
+        ],
         compiler_params=pltpu.CompilerParams(vmem_limit_bytes=60 * 1024 * 1024),
     )(moved)
 

time: 42.5 us -> 24.1 us (0.57)
  Pallas kernels: 42.4 us -> 23.9 us
    pallas_call x1, Pallas kernels: 20 us -> 1.87 us  [body(): pl.pallas_call(functools.partial(hand_over, chunks), out_shape=jax.ShapeD...]
where the time goes in v2:
time: 24.1 us; the launch traced here: 23.9 us
  Pallas kernels  23.9 us (99%)
    pallas_call x1, Pallas kernels, body(): pl.pallas_call(functools.partial(kernel, (n_gx, n_gy, n_gz, steps)), out_...  22 us
    pallas_call x1, Pallas kernels, body(): pl.pallas_call(functools.partial(hand_over, chunks), out_shape=jax.ShapeD...  1.87 us

profile of v2, /device:TPU:0, one launch (start us, length us, event | category | flops | bytes accessed | tf_op | source)
XLA Modules:
  0.0 23.9 jit_solution(5757623357087241265)
XLA Ops:
  0.0 22.0 %shard_map.46.source = f32[19,8,8,128]{3,2,1,0:T(8,128)} custom-call(s32[2,2]{1,0:T(2,128)} %off_in.1, s32[2,2]{1,0:T(2,128)} %frac_in.1, f32[19,8,8,128]{3,2,1,0:T(8,128)} %pops_in.1, s32[8,8,128]{2,1,0:T(8,128)} %codes_in.1), custom_call_target="tpu_custom_call" | custom-call | tf_op jit(solution)/shard_map/pallas_call | solution.py:436
  22.0 1.9 %shard_map.47 = f32[19,8,8,128]{3,2,1,0:T(8,128)} custom-call(f32[19,8,8,128]{3,2,1,0:T(8,128)} %shard_map.46.source), custom_call_target="tpu_custom_call" | custom-call | tf_op jit(solution)/shard_map/pallas_call | solution.py:475

commit v3 on v2

--- a/solution.py
+++ b/solution.py
@@ -81,14 +81,14 @@
 
 
 def kernel(
-    sizes, off_in, frac_in, pops_in, codes_in, out_to,
-    off, frac, pops, codes, out, load_sem, save_sem,
+    sizes, pops, codes, out,
+    table, table_sem,
     post, s_strip, s_inner, s_end, s_col, s_corner, s_edge,
     r_inner, r_end, r_col, r_corner, r_edge, send_sem, recv_sem, *gathers
 ):
     n_gx, n_gy, n_gz, steps = sizes
     r_strip = [gathers[2 * step : 2 * step + 2] for step in range(steps)]
-    layers, rows, cols = codes.shape
+    _, layers, rows, cols = pops.shape
     length = n_gx * rows
     top = layers - 1
     gx, gy, gz = lax.axis_index("gx"), lax.axis_index("gy"), lax.axis_index("gz")
@@ -169,22 +169,8 @@
             if entry[0] in groups:
                 copy_of(step, number, entry, False).wait_send()
 
-    inside = pl.ds(1, layers - 2)
-    loads = [
-        pltpu.make_async_copy(src, dst, load_sem.at[number])
-        for number, (src, dst) in enumerate(
-            (
-                (codes_in, codes),
-                (pops_in.at[:, 0], pops.at[:, 0]),
-                (pops_in.at[:, top], pops.at[:, top]),
-                (pops_in.at[:, inside], pops.at[:, inside]),
-                (off_in, off),
-                (frac_in, frac),
-            )
-        )
-    ]
-    for load in loads:
-        load.start()
+    load_table = pltpu.make_async_copy(codes.at[pl.ds(layers * rows, rows)], table, table_sem)
+    load_table.start()
 
     moves = sorted({tuple(m % n for m, n in zip(entry[1], (n_gx, n_gy, n_gz))) for entry in messages(0)})
     barrier = pltpu.get_barrier_semaphore()
@@ -247,15 +233,15 @@
         dx, dy, _ = velocities[i]
         if side == 0:
             plane = gz
-            near = gx * rows - dx - off[step, plane]
+            near = gx * rows - dx - table[step, plane]
             far = near - 1
         else:
             plane = lax.rem(gz + 1, n_gz)
-            near = gx * rows - dx + off[step, plane]
+            near = gx * rows - dx + table[step, plane]
             far = near + 1
         near = lax.rem(near + 2 * length, length)
         far = lax.rem(far + 2 * length, length)
-        weight = frac[step, plane].astype(jnp.float32) * (1.0 / FRAC_DEN)
+        weight = table[steps + step, plane].astype(jnp.float32) * (1.0 / FRAC_DEN)
         value = (1.0 - weight) * r_strip[step][side][j, pl.ds(near, rows), :]
         value = value + weight * r_strip[step][side][j, pl.ds(far, rows), :]
         if dy == 0:
@@ -328,29 +314,25 @@
 
     packed = nothing
     ends = {}
-    loads[0].wait()
-    for number, z in ((1, 0), (2, top)):
-        loads[number].wait()
-        ends[z] = collide([pops[i, z] for i in range(19)], codes[z])
+    for z in (0, top):
+        ends[z] = collide([pops[i, z] for i in range(19)], codes[z * rows : (z + 1) * rows])
         packed = publish(0, z, ends[z], packed)
     publish_strip(0, 0, ends[top])
     publish_strip(0, 1, ends[0])
     publish_edges(0, ends[0], ends[top])
     pl.semaphore_wait(barrier, len(moves))
+    start(0, "rise")
     start(0, "edge")
-    start(0, "rise")
-    loads[3].wait()
 
     def first(z, packed):
-        return publish(0, z, collide([pops[i, z] for i in range(19)], codes[z]), packed)
+        return publish(0, z, collide([pops[i, z] for i in range(19)], codes[z * rows : (z + 1) * rows]), packed)
 
     publish_columns(0, inner(first, packed))
     start(0, "inner")
     start(0, "near")
     finish(0, ("rise",))
     start(0, "sink")
-    loads[4].wait()
-    loads[5].wait()
+    load_table.wait()
 
     for step in range(1, steps):
         arrive(step - 1, "inner")
@@ -358,20 +340,20 @@
         halos = halo_columns(step - 1)
 
         def middle(z, packed, step=step, halos=halos):
-            return publish(step, z, collide(passed(step - 1, z, halos, None), codes[z]), packed)
+            return publish(step, z, collide(passed(step - 1, z, halos, None), codes[z * rows : (z + 1) * rows]), packed)
 
         packed = inner(middle, nothing)
         start(step, "inner")
         arrive(step - 1, "edge")
         arrive(step - 1, "rise")
         wrap_rows(step - 1, 0)
-        ends[0] = collide(passed(step - 1, 0, halos, 0), codes[0])
+        ends[0] = collide(passed(step - 1, 0, halos, 0), codes[:rows])
         publish_strip(step, 1, ends[0])
         start(step, "sink")
         packed = publish(step, 0, ends[0], packed)
         arrive(step - 1, "sink")
         wrap_rows(step - 1, 1)
-        ends[top] = collide(passed(step - 1, top, halos, top), codes[top])
+        ends[top] = collide(passed(step - 1, top, halos, top), codes[top * rows : layers * rows])
         publish_strip(step, 0, ends[top])
         publish_edges(step, ends[0], ends[top])
         start(step, "edge")
@@ -390,38 +372,15 @@
         return carry
 
     inner(last, 0)
-    saves = [pltpu.make_async_copy(out.at[:, inside], out_to.at[:, inside], save_sem.at[0])]
-    saves[0].start()
     arrive(step, "edge")
     for side, z in ((1, top), (0, 0)):
         arrive(step, ("rise", "sink")[side])
         wrap_rows(step, side)
         for i, value in enumerate(passed(step, z, halos, z)):
             out[i, z] = value
-        saves.append(pltpu.make_async_copy(out.at[:, z], out_to.at[:, z], save_sem.at[len(saves)]))
-        saves[-1].start()
     finish(0, ("sink", "inner", "near", "edge"))
     for step in range(1, steps):
         finish(step, ("rise", "sink", "inner", "near", "edge"))
-    for save in saves:
-        save.wait()
-
-
-def hand_over(chunks, source, target, held, load_sem, save_sem):
-    count = source.shape[0]
-    cuts = [count * c // chunks for c in range(chunks + 1)]
-    loads, saves = [], []
-    for c in range(chunks):
-        part = pl.ds(cuts[c], cuts[c + 1] - cuts[c])
-        loads.append(pltpu.make_async_copy(source.at[part], held.at[part], load_sem.at[c]))
-        saves.append(pltpu.make_async_copy(held.at[part], target.at[part], save_sem.at[c]))
-    for load in loads:
-        load.start()
-    for load, save in zip(loads, saves):
-        load.wait()
-        save.start()
-    for save in saves:
-        save.wait()
 
 
 def body(sizes, populations, solid_codes, plane_offsets, plane_fractions):
@@ -433,24 +392,23 @@
     n_messages = 2 * n_gx + 2 * 2 + 2 + 4 + n_z * 2 * n_gx
     inner_rows = -(-5 * (layers - 2) // 8) * 8
     f32 = jnp.float32
-    moved = pl.pallas_call(
+    planes = plane_offsets.shape[1]
+    beyond = cols - planes
+    cells = layers * rows
+    codes = jnp.pad(solid_codes.reshape(cells, cols), ((0, rows), (0, 0)))
+    codes += jnp.pad(plane_offsets, ((cells, rows - steps), (0, beyond)))
+    codes += jnp.pad(plane_fractions, ((cells + steps, rows - 2 * steps), (0, beyond)))
+    return pl.pallas_call(
         functools.partial(kernel, (n_gx, n_gy, n_gz, steps)),
         out_shape=jax.ShapeDtypeStruct(populations.shape, f32),
         in_specs=[
-            pl.BlockSpec(memory_space=pltpu.HBM),
-            pl.BlockSpec(memory_space=pltpu.HBM),
-            pl.BlockSpec(memory_space=pltpu.HBM),
-            pl.BlockSpec(memory_space=pltpu.HBM),
+            pl.BlockSpec(memory_space=pltpu.VMEM),
+            pl.BlockSpec(memory_space=pltpu.VMEM),
         ],
-        out_specs=pl.BlockSpec(memory_space=pltpu.HBM),
+        out_specs=pl.BlockSpec(memory_space=pltpu.VMEM),
         scratch_shapes=[
-            pltpu.SMEM(plane_offsets.shape, jnp.int32),
-            pltpu.SMEM(plane_fractions.shape, jnp.int32),
-            pltpu.VMEM(populations.shape, f32),
-            pltpu.VMEM(solid_codes.shape, jnp.int32),
-            pltpu.VMEM(populations.shape, f32),
-            pltpu.SemaphoreType.DMA((6,)),
-            pltpu.SemaphoreType.DMA((3,)),
+            pltpu.SMEM((rows, cols), jnp.int32),
+            pltpu.SemaphoreType.DMA(()),
             pltpu.VMEM((steps, 19, layers, rows, cols), f32),
             pltpu.VMEM((steps, 2, 5, rows, cols), f32),
             pltpu.VMEM((steps, 2, inner_rows, cols), f32),
@@ -468,22 +426,9 @@
         ]
         + [pltpu.VMEM((5, gathered, cols), f32)] * (2 * steps),
         compiler_params=pltpu.CompilerParams(
-            collective_id=0, has_side_effects=True, vmem_limit_bytes=60 * 1024 * 1024
+            collective_id=0, has_side_effects=True, vmem_limit_bytes=32 * 1024 * 1024
         ),
-    )(plane_offsets, plane_fractions, populations, solid_codes)
-    chunks = 4
-    return pl.pallas_call(
-        functools.partial(hand_over, chunks),
-        out_shape=jax.ShapeDtypeStruct(populations.shape, f32),
-        in_specs=[pl.BlockSpec(memory_space=pltpu.HBM)],
-        out_specs=pl.BlockSpec(memory_space=pltpu.HBM),
-        scratch_shapes=[
-            pltpu.VMEM(populations.shape, f32),
-            pltpu.SemaphoreType.DMA((chunks,)),
-            pltpu.SemaphoreType.DMA((chunks,)),
-        ],
-        compiler_params=pltpu.CompilerParams(vmem_limit_bytes=60 * 1024 * 1024),
-    )(moved)
+    )(populations, codes)
 
 
 def solution(mesh):

time: 24.1 us -> 25 us (1.037)
  local copies, waits for them, and re-layouts: 0 us -> 2.58 us
  Pallas kernels: 23.9 us -> 21.4 us
  other arithmetic: 0 us -> 0.78 us
    unnamed x0 -> x5, local copies, waits for them, and re-layouts: none -> 2.58 us
    pallas_call x1 -> x0, Pallas kernels: 1.87 us -> none  [body(): pl.pallas_call(functools.partial(hand_over, chunks), out_shape=jax.ShapeD...]
    add x0 -> x1, other arithmetic: none -> 0.78 us  [body(): codes += jnp.pad(plane_fractions, ((cells + steps, rows - 2 * steps), (0,...]
    pallas_call x1, Pallas kernels: 22 us -> 21.4 us  [body(): pl.pallas_call(functools.partial(kernel, (n_gx, n_gy, n_gz, steps)), out_...]
where the time goes in v3:
time: 25 us; the launch traced here: 24.8 us
  Pallas kernels  21.4 us (86%)
  local copies, waits for them, and re-layouts  2.58 us (10%)
  other arithmetic  0.78 us (3%)
    pallas_call x1, Pallas kernels, body(): pl.pallas_call(functools.partial(kernel, (n_gx, n_gy, n_gz, steps)), out_...  21.4 us
    unnamed x5, local copies, waits for them, and re-layouts  2.58 us
    add x1, other arithmetic, body(): codes += jnp.pad(plane_fractions, ((cells + steps, rows - 2 * steps), (0,...  0.78 us

profile of v3, /device:TPU:0, one launch (start us, length us, event | category | flops | bytes accessed | tf_op | source)
XLA Modules:
  0.0 24.8 jit_solution(3462556139099381565)
XLA Ops:
  0.0 0.0 copy-start.1
  0.0 0.7 %copy-done.1 = s32[2,2]{1,0:T(2,128)S(1)} copy-done((s32[2,2]{1,0:T(2,128)S(1)}, s32[2,2]{1,0:T(2,128)}, u32[]{:S(2)}) %copy-start.1) | copy-done | bytes 40
  0.7 0.8 %pad_add_fusion.codes = s32[72,128]{1,0:T(8,128)S(1)} fusion(s32[2,2]{1,0:T(2,128)S(1)} %copy-done.1, s32[2,2]{1,0:T(2,128)} %param.6, s32[64,128]{1,0:T(8,128)} %bitcast.1), kind=kLoop, calls=%fused_computation | loop fusion | flops 18432 | bytes 69664 | tf_op jit(solution)/shard_map/add | solution.py:400
  1.5 0.0 copy-start
  1.5 1.1 %copy-done = f32[19,8,8,128]{3,2,1,0:T(8,128)S(1)} copy-done((f32[19,8,8,128]{3,2,1,0:T(8,128)S(1)}, f32[19,8,8,128]{3,2,1,0:T(8,128)}, u32[]{:S(2)}) %copy-start) | copy-done | bytes 622616
  2.5 21.4 %shard_map.46 = f32[19,8,8,128]{3,2,1,0:T(8,128)S(1)} custom-call(f32[19,8,8,128]{3,2,1,0:T(8,128)S(1)} %copy-done, s32[72,128]{1,0:T(8,128)S(1)} %pad_add_fusion.codes), custom_call_target="tpu_custom_call" | custom-call | tf_op jit(solution)/shard_map/pallas_call | solution.py:401
  23.9 0.8 %copy.6 = f32[19,8,8,128]{3,2,1,0:T(8,128)} copy(f32[19,8,8,128]{3,2,1,0:T(8,128)S(1)} %shard_map.46) | data formatting | bytes 1245184
Async XLA Ops:
  0.0 0.7 %copy-start.1 = (s32[2,2]{1,0:T(2,128)S(1)}, s32[2,2]{1,0:T(2,128)}, u32[]{:S(2)}) copy-start(s32[2,2]{1,0:T(2,128)} %param.7) | copy-start | bytes 52
  1.5 1.1 %copy-start = (f32[19,8,8,128]{3,2,1,0:T(8,128)S(1)}, f32[19,8,8,128]{3,2,1,0:T(8,128)}, u32[]{:S(2)}) copy-start(f32[19,8,8,128]{3,2,1,0:T(8,128)} %pops.1) | copy-start | bytes 1867780

commit v4 on v2

--- a/solution.py
+++ b/solution.py
@@ -84,7 +84,7 @@
     sizes, off_in, frac_in, pops_in, codes_in, out_to,
     off, frac, pops, codes, out, load_sem, save_sem,
     post, s_strip, s_inner, s_end, s_col, s_corner, s_edge,
-    r_inner, r_end, r_col, r_corner, r_edge, send_sem, recv_sem, *gathers
+    r_inner, r_end, r_col, r_corner, r_edge, send_sem, recv_sem, relay_sem, *gathers
 ):
     n_gx, n_gy, n_gz, steps = sizes
     r_strip = [gathers[2 * step : 2 * step + 2] for step in range(steps)]
@@ -154,20 +154,82 @@
             device_id_type=MESH,
         )
 
+    relayed = n_gx == 4
+    relays = ((2, 1, 0, 3), (1, -1, 3, 1)) if relayed else ()
+    strip_order = (2, 3, 1, 0) if relayed else tuple(range(n_gx))
+
+    def strip_numbers(group):
+        base = 0 if group == "rise" else n_gx
+        return [base + k for k in strip_order]
+
+    def for_strip(number, act):
+        distance = number % n_gx
+        if relayed and distance in (1, 3):
+            pl.when(gx != (3 if distance == 1 else 0))(act)
+        else:
+            act()
+
     def start(step, group):
-        for number, entry in enumerate(messages(step)):
+        entries = messages(step)
+        if group in ("rise", "sink"):
+            for number in strip_numbers(group):
+                for_strip(number, lambda number=number: copy_of(step, number, entries[number], False).start())
+            return
+        for number, entry in enumerate(entries):
             if entry[0] == group:
                 copy_of(step, number, entry, False).start()
 
-    def arrive(step, group):
+    def arrive(step, group, skip=None):
         for number, entry in enumerate(messages(step)):
-            if entry[0] == group:
+            if entry[0] == group and number != skip:
                 copy_of(step, number, entry, True).wait_recv()
 
+    def relay_copy(step, side, relay):
+        _, move, slot, distance = relay
+        block = r_strip[step][side].at[:, pl.ds(slot * rows, rows), :]
+        return pltpu.make_async_remote_copy(
+            src_ref=block,
+            dst_ref=block,
+            send_sem=relay_sem.at[step, side],
+            recv_sem=recv_sem.at[step, side * n_gx + distance],
+            device_id=peer((move, 0, 0)),
+            device_id_type=MESH,
+        )
+
+    def forward(step, side):
+        if not relayed:
+            return
+        number = side * n_gx + 2
+
+        def pass_on(relay):
+            copy_of(step, number, messages(step)[number], True).wait_recv()
+            relay_copy(step, side, relay).start()
+
+        for relay in relays:
+            pl.when(gx == relay[0])(functools.partial(pass_on, relay))
+
+    def arrive_rest(step, side):
+        number = side * n_gx + 2 if relayed else None
+        arrive(step, ("rise", "sink")[side], number)
+        if relayed:
+            at_end = (gx == 0) | (gx == n_gx - 1)
+            pl.when(at_end)(lambda: copy_of(step, number, messages(step)[number], True).wait_recv())
+
     def finish(step, groups):
-        for number, entry in enumerate(messages(step)):
-            if entry[0] in groups:
-                copy_of(step, number, entry, False).wait_send()
+        entries = messages(step)
+        for group in groups:
+            if group in ("rise", "sink"):
+                for number in strip_numbers(group):
+                    for_strip(number, lambda number=number: copy_of(step, number, entries[number], False).wait_send())
+                continue
+            for number, entry in enumerate(entries):
+                if entry[0] == group:
+                    copy_of(step, number, entry, False).wait_send()
+
+    def finish_relays(step):
+        for side in (0, 1):
+            for relay in relays:
+                pl.when(gx == relay[0])(lambda relay=relay, side=side: relay_copy(step, side, relay).wait_send())
 
     inside = pl.ds(1, layers - 2)
     loads = [
@@ -337,8 +399,8 @@
     publish_strip(0, 1, ends[0])
     publish_edges(0, ends[0], ends[top])
     pl.semaphore_wait(barrier, len(moves))
+    start(0, "rise")
     start(0, "edge")
-    start(0, "rise")
     loads[3].wait()
 
     def first(z, packed):
@@ -356,20 +418,22 @@
         arrive(step - 1, "inner")
         arrive(step - 1, "near")
         halos = halo_columns(step - 1)
+        forward(step - 1, 0)
 
         def middle(z, packed, step=step, halos=halos):
             return publish(step, z, collide(passed(step - 1, z, halos, None), codes[z]), packed)
 
         packed = inner(middle, nothing)
         start(step, "inner")
+        forward(step - 1, 1)
         arrive(step - 1, "edge")
-        arrive(step - 1, "rise")
+        arrive_rest(step - 1, 0)
         wrap_rows(step - 1, 0)
         ends[0] = collide(passed(step - 1, 0, halos, 0), codes[0])
         publish_strip(step, 1, ends[0])
         start(step, "sink")
         packed = publish(step, 0, ends[0], packed)
-        arrive(step - 1, "sink")
+        arrive_rest(step - 1, 1)
         wrap_rows(step - 1, 1)
         ends[top] = collide(passed(step - 1, top, halos, top), codes[top])
         publish_strip(step, 0, ends[top])
@@ -383,6 +447,7 @@
     arrive(step, "inner")
     arrive(step, "near")
     halos = halo_columns(step)
+    forward(step, 1)
 
     def last(z, carry):
         for i, value in enumerate(passed(step, z, halos, None)):
@@ -392,9 +457,10 @@
     inner(last, 0)
     saves = [pltpu.make_async_copy(out.at[:, inside], out_to.at[:, inside], save_sem.at[0])]
     saves[0].start()
+    forward(step, 0)
     arrive(step, "edge")
     for side, z in ((1, top), (0, 0)):
-        arrive(step, ("rise", "sink")[side])
+        arrive_rest(step, side)
         wrap_rows(step, side)
         for i, value in enumerate(passed(step, z, halos, z)):
             out[i, z] = value
@@ -403,6 +469,8 @@
     finish(0, ("sink", "inner", "near", "edge"))
     for step in range(1, steps):
         finish(step, ("rise", "sink", "inner", "near", "edge"))
+    for step in range(steps):
+        finish_relays(step)
     for save in saves:
         save.wait()
 
@@ -465,6 +533,7 @@
             pltpu.VMEM((steps, n_z, 2, n_gx, 1, cols), f32),
             pltpu.SemaphoreType.DMA((steps, n_messages)),
             pltpu.SemaphoreType.DMA((steps, n_messages)),
+            pltpu.SemaphoreType.DMA((steps, 2)),
         ]
         + [pltpu.VMEM((5, gathered, cols), f32)] * (2 * steps),
         compiler_params=pltpu.CompilerParams(

time: 24.1 us -> 27.1 us (1.12)
  Pallas kernels: 23.9 us -> 26.9 us
    pallas_call x1, Pallas kernels: 22 us -> 25 us  [body(): pl.pallas_call(functools.partial(kernel, (n_gx, n_gy, n_gz, steps)), out_...]
where the time goes in v4:
time: 27.1 us; the launch traced here: 26.9 us
  Pallas kernels  26.9 us (99%)
    pallas_call x1, Pallas kernels, body(): pl.pallas_call(functools.partial(kernel, (n_gx, n_gy, n_gz, steps)), out_...  25 us
    pallas_call x1, Pallas kernels, body(): pl.pallas_call(functools.partial(hand_over, chunks), out_shape=jax.ShapeD...  1.87 us

profile of v4, /device:TPU:0, one launch (start us, length us, event | category | flops | bytes accessed | tf_op | source)
XLA Modules:
  0.0 26.9 jit_solution(13228070945377386675)
XLA Ops:
  0.0 25.0 %shard_map.46.source = f32[19,8,8,128]{3,2,1,0:T(8,128)} custom-call(s32[2,2]{1,0:T(2,128)} %off_in.1, s32[2,2]{1,0:T(2,128)} %frac_in.1, f32[19,8,8,128]{3,2,1,0:T(8,128)} %pops_in.1, s32[8,8,128]{2,1,0:T(8,128)} %codes_in.1), custom_call_target="tpu_custom_call" | custom-call | tf_op jit(solution)/shard_map/pallas_call | solution.py:504
  25.0 1.9 %shard_map.47 = f32[19,8,8,128]{3,2,1,0:T(8,128)} custom-call(f32[19,8,8,128]{3,2,1,0:T(8,128)} %shard_map.46.source), custom_call_target="tpu_custom_call" | custom-call | tf_op jit(solution)/shard_map/pallas_call | solution.py:544

commit v5 on v2

--- a/solution.py
+++ b/solution.py
@@ -337,7 +337,6 @@
     publish_strip(0, 1, ends[0])
     publish_edges(0, ends[0], ends[top])
     pl.semaphore_wait(barrier, len(moves))
-    start(0, "edge")
     start(0, "rise")
     loads[3].wait()
 
@@ -347,6 +346,7 @@
     publish_columns(0, inner(first, packed))
     start(0, "inner")
     start(0, "near")
+    start(0, "edge")
     finish(0, ("rise",))
     start(0, "sink")
     loads[4].wait()
@@ -373,11 +373,11 @@
         wrap_rows(step - 1, 1)
         ends[top] = collide(passed(step - 1, top, halos, top), codes[top])
         publish_strip(step, 0, ends[top])
-        publish_edges(step, ends[0], ends[top])
-        start(step, "edge")
         start(step, "rise")
         publish_columns(step, publish(step, top, ends[top], packed))
         start(step, "near")
+        publish_edges(step, ends[0], ends[top])
+        start(step, "edge")
 
     step = steps - 1
     arrive(step, "inner")
@@ -471,7 +471,7 @@
             collective_id=0, has_side_effects=True, vmem_limit_bytes=60 * 1024 * 1024
         ),
     )(plane_offsets, plane_fractions, populations, solid_codes)
-    chunks = 4
+    chunks = 10
     return pl.pallas_call(
         functools.partial(hand_over, chunks),
         out_shape=jax.ShapeDtypeStruct(populations.shape, f32),

time: 24.1 us -> 24.5 us (1.017)
  Pallas kernels: 23.9 us -> 24.3 us
    pallas_call x1, Pallas kernels: 22 us -> 22.4 us  [body(): pl.pallas_call(functools.partial(kernel, (n_gx, n_gy, n_gz, steps)), out_...]
where the time goes in v5:
time: 24.5 us; the launch traced here: 24.3 us
  Pallas kernels  24.3 us (99%)
    pallas_call x1, Pallas kernels, body(): pl.pallas_call(functools.partial(kernel, (n_gx, n_gy, n_gz, steps)), out_...  22.4 us
    pallas_call x1, Pallas kernels, body(): pl.pallas_call(functools.partial(hand_over, chunks), out_shape=jax.ShapeD...  1.92 us

profile of v5, /device:TPU:0, one launch (start us, length us, event | category | flops | bytes accessed | tf_op | source)
XLA Modules:
  0.0 24.3 jit_solution(17212765914861908091)
XLA Ops:
  0.0 22.4 %shard_map.46.source = f32[19,8,8,128]{3,2,1,0:T(8,128)} custom-call(s32[2,2]{1,0:T(2,128)} %off_in.1, s32[2,2]{1,0:T(2,128)} %frac_in.1, f32[19,8,8,128]{3,2,1,0:T(8,128)} %pops_in.1, s32[8,8,128]{2,1,0:T(8,128)} %codes_in.1), custom_call_target="tpu_custom_call" | custom-call | tf_op jit(solution)/shard_map/pallas_call | solution.py:436
  22.4 1.9 %shard_map.47 = f32[19,8,8,128]{3,2,1,0:T(8,128)} custom-call(f32[19,8,8,128]{3,2,1,0:T(8,128)} %shard_map.46.source), custom_call_target="tpu_custom_call" | custom-call | tf_op jit(solution)/shard_map/pallas_call | solution.py:475
